TPU v7x, 128 devices: a whole 4x4x4 slice. The times are simulated.
128 devices in a mesh: hold: 16 (over y, x_hi, core), bulk: 8 (over z, x_lo).
Axes of the slice: x: 4 (x_hi: 2, x_lo: 2; x = x_hi * 2 + x_lo), y: 4, z: 4, core: 2. Of those that a mesh axis runs over, the one named last changes fastest.
Arguments:
- queries: bfloat16 [2048, 8192], P(('hold', 'bulk')), may hold values from -12 to 12
- out_grad: bfloat16 [2048, 8192], P(('hold', 'bulk')), may hold values from -48 to 48
- attn_out: bfloat16 [2048, 8192], P(('hold', 'bulk')), may hold values from -3 to 3
- log_totals: float32 [2048, 64], P('hold', 'bulk'), may hold values from 11 to 13
- prompt_keys: bfloat16 [16384, 1024], P('hold', 'bulk'), may hold values from -6 to 6
- prompt_values: bfloat16 [16384, 1024], P('hold', 'bulk'), may hold values from -6 to 6
- rollout_keys: bfloat16 [2048, 1024], P('hold', 'bulk'), may hold values from -6 to 6
- rollout_values: bfloat16 [2048, 1024], P('hold', 'bulk'), may hold values from -6 to 6
- rollout_blocks: int32 [8], replicated, may hold values from 1 to 4, 16 in all
Outputs:
- query_grad: bfloat16 [2048, 8192], P(('hold', 'bulk'))
- prompt_key_grad: float32 [16384, 1024], P('hold', 'bulk')
- prompt_value_grad: float32 [16384, 1024], P('hold', 'bulk')
- rollout_key_grad: float32 [2048, 1024], P('hold', 'bulk')
- rollout_value_grad: float32 [2048, 1024], P('hold', 'bulk')
Inputs may be any that keep to these rules, and one draw needn't show every extreme that they name: `rollout_blocks`: the entries sum to 16; the largest is exactly 4.
All inputs are finite; a program needn't handle non-finite values.
Results may differ from a plain program's by a relative error of at most 0.0055.
Values may be sent and summed in bfloat16 or wider, within the bound.
No kernel may reach another device: no remote copies, remote signals or barrier semaphores. Data moves between devices by JAX's collectives and lax.ppermute only.
A program may use at most 128 MiB of HBM per device.

v0:
```python
import functools

import jax
import jax.numpy as jnp
from jax import lax
from jax.experimental import pallas as pl
from jax.experimental.pallas import tpu as pltpu
from jax.sharding import Mesh
from jax.sharding import PartitionSpec as P

F32 = jnp.float32
BF16 = jnp.bfloat16
HD = 128
GROUP = 8
BLOCK = 128
NBLK = 16
PK = 1024
RK = 128
KW = PK + RK
QR = BLOCK * GROUP
SRC = 8
SUB = BLOCK // SRC
DROW = 2 * BLOCK
LROW = DROW + 8
PAY = LROW + 8
SCALE = HD ** (-0.5)
LOG2E = 1.4426950408889634
C2 = SCALE * LOG2E

NN = (((1,), (0,)), ((), ()))
NT = (((1,), (1,)), ((), ()))

Y, XH, C, Z, XL = "y", "xh", "c", "z", "xl"
BULK = (Z, XL)


def dot(a, b, dims):
    return lax.dot_general(a, b, dims, preferred_element_type=F32)


def held(*arrays):
    return [pltpu.with_memory_space_constraint(a, pltpu.VMEM) for a in arrays]


ANYSPEC = pl.BlockSpec(memory_space=pl.ANY)
VSPEC = pl.BlockSpec(memory_space=pltpu.VMEM)
SSPEC = pl.BlockSpec(memory_space=pltpu.SMEM)


def pieces_of(x):
    a = x.astype(BF16).astype(F32)
    b = (x - a).astype(BF16).astype(F32)
    return a, b, x - a - b


def pack_kernel(place, q_in, g_in, o_in, pay, q, g, o, sems):
    loads = [
        pltpu.make_async_copy(src, dst, sems.at[n])
        for n, (src, dst) in enumerate(((q_in, q), (g_in, g), (o_in, o)))
    ]
    for copy in loads:
        copy.start()
    for copy in loads:
        copy.wait()
    ones = jnp.ones((16, HD), BF16)
    row = lax.broadcasted_iota(jnp.int32, (16, BLOCK), 0)
    for b in range(SRC):
        prods = []
        for h in range(GROUP):
            cols = slice((b * GROUP + h) * HD, (b * GROUP + h + 1) * HD)
            qh, gh = q[:, cols], g[:, cols]
            pay[b, h * SUB : (h + 1) * SUB, :] = qh
            pay[b, BLOCK + h * SUB : BLOCK + (h + 1) * SUB, :] = gh
            prods.append(gh.astype(F32) * o[:, cols].astype(F32))
        prod = jnp.concatenate(prods, axis=0)
        high = prod.astype(BF16)
        low = (prod - high.astype(F32)).astype(BF16)
        d1, d2, d3 = pieces_of(dot(ones, high, NT) + dot(ones, low, NT))
        rows = jnp.where(row == 0, d1, jnp.where(row == 1, d2, jnp.where(row == 2, d3, 0.0)))
        pay[b, DROW:PAY, :] = rows.astype(BF16)


def in_hbm(arrays):
    return [pltpu.with_memory_space_constraint(a, pltpu.HBM) for a in arrays]


def pack(place, *arrays):
    return pl.pallas_call(
        pack_kernel,
        in_specs=[SSPEC] + [ANYSPEC] * 3,
        out_specs=VSPEC,
        out_shape=pltpu.VMEM((SRC, PAY, HD), BF16),
        scratch_shapes=[pltpu.VMEM((SUB, SRC * GROUP * HD), BF16)] * 3
        + [pltpu.SemaphoreType.DMA((3,))],
        compiler_params=pltpu.CompilerParams(vmem_limit_bytes=8 << 20),
        name="pack",
    )(place, *in_hbm(arrays))


def join_kernel(pk, rk, pv, rv, kv, sems):
    copies, at = [], 0
    for n, (src, rows) in enumerate(((pk, PK), (rk, RK), (pv, PK), (rv, RK))):
        copies.append(pltpu.make_async_copy(src, kv.at[pl.ds(at, rows)], sems.at[n]))
        at += rows
    for copy in copies:
        copy.start()
    for copy in copies:
        copy.wait()


def join(*arrays):
    return pl.pallas_call(
        join_kernel,
        in_specs=[ANYSPEC] * 4,
        out_specs=VSPEC,
        out_shape=pltpu.VMEM((2 * KW, HD), BF16),
        scratch_shapes=[pltpu.SemaphoreType.DMA((4,))],
        compiler_params=pltpu.CompilerParams(vmem_limit_bytes=4 << 20),
        name="join",
    )(*in_hbm(arrays))


def column(rows):
    line = jnp.concatenate([rows[s : s + 1, :] for s in range(SRC)], axis=1)
    return jnp.broadcast_to(line, (HD, QR)).T


def tiles_kernel(cfg, *refs):
    unit, keys_of, have_sums, have_dq, final, others = cfg
    nk = len(keys_of)
    refs = list(refs)

    def take(n):
        out = refs[:n]
        del refs[:n]
        return out

    place, lengths = take(2)
    pays = take(2 if unit == "near" else 1)
    rows_all = QR * len(pays)
    keys = take(nk)
    sums_in = [take(1)[0] if h else None for h in have_sums]
    dq_in = take(1)[0] if have_dq else None
    blocks = take(others)
    sums = take(nk)
    dq_out, qs, gs, qt, gt, log_col, delta_col, dqa, done, sems = refs
    dq = dqa if final else dq_out
    copies = []
    if blocks:
        parts = ((0, blocks[0]), (1, blocks[1].at[0]), (3, blocks[1].at[1]))
        for n, (back, block) in enumerate(parts):
            target = dq_out.at[(place[0] + back) % 4]
            copies.append(pltpu.make_async_copy(block, target, sems.at[n]))
    for copy in copies:
        copy.start()

    for m, pay in enumerate(pays):
        rows = slice(m * QR, (m + 1) * QR)
        qs[rows, :] = pay[:, 0:BLOCK, :].reshape(QR, HD)
        gs[rows, :] = pay[:, BLOCK : 2 * BLOCK, :].reshape(QR, HD)
        scalars = pay[:, DROW:PAY, :].astype(F32)
        add3 = lambda n: scalars[:, n, :] + scalars[:, n + 1, :] + scalars[:, n + 2, :]
        delta_col[rows, :] = column(add3(0))
        log_col[rows, :] = column(add3(LROW - DROW))
    qt[...] = qs[...].T
    gt[...] = gs[...].T
    for j in range(nk):
        tail = sums_in[j][:, PK:KW] if have_sums[j] else jnp.zeros((2 * HD, RK), F32)
        sums[j][:, PK:KW] = tail

    def products(j, at, width, rows):
        s = dot(qs[:rows], keys[j][pl.ds(at, width), :], NT)
        dp = dot(gs[:rows], keys[j][pl.ds(KW + at, width), :], NT)
        return s, dp

    def grads(j, at, width, rows, s, dp, allowed, old):
        wide = lambda col: jnp.concatenate([col[:rows]] * (width // HD), axis=1)
        p = jnp.exp2(s * C2 - wide(log_col))
        if allowed is not None:
            p = jnp.where(allowed, p, 0.0)
        ds = (p * (dp - wide(delta_col))).astype(BF16)
        p = p.astype(BF16)
        cols = pl.ds(at, width)
        for half, left, right in ((slice(0, HD), qt, ds), (slice(HD, 2 * HD), gt, p)):
            term = dot(left[:, :rows], right, NN)
            sums[j][half, cols] = term if old is None else old[half, cols] + term
        return dot(ds, keys[j][pl.ds(at, width), :], NN)

    dq[...] = jnp.zeros((rows_all, HD), F32) if dq_in is None else dq_in[...]
    part = 256
    steps = 2 if unit == "near" else 2 if nk == 2 else 1

    def step(n, carry):
        total = None
        chunks = [
            (j, at if steps == 1 else pl.multiple_of(n * (PK // steps) + at, part))
            for j in range(nk)
            for at in range(0, PK // steps, part)
        ]
        ahead = products(*chunks[0], part, rows_all)
        for m, (j, at) in enumerate(chunks):
            s, dp = ahead
            if m + 1 < len(chunks):
                ahead = products(*chunks[m + 1], part, rows_all)
            term = grads(j, at, part, rows_all, s, dp, None, sums_in[j])
            total = term if total is None else total + term
        dq[...] += total
        return carry

    if steps == 1:
        step(0, 0)
    else:
        lax.fori_loop(0, steps, step, 0)

    if unit != "opp":
        y, xh, c = place[0], place[1], place[2]
        qi = 4 * (y if unit == "own" else (y + 1) % 4) + 2 * xh + c
        for j, (other_chip, other_core) in enumerate(keys_of):
            kj = 4 * y + 2 * ((1 - xh) if other_chip else xh) + ((1 - c) if other_core else c)
            seen, end = kj <= qi, 0
            for r in range(lengths.shape[0]):
                end = end + lengths[r]
                seen = seen & ((end <= kj) | (end > qi))

            @pl.when(seen)
            def _():
                allowed = None
                if unit == "own":
                    row = lax.broadcasted_iota(jnp.int32, (QR, RK), 0)
                    key_at = lax.broadcasted_iota(jnp.int32, (QR, RK), 1)
                    token = (row // BLOCK) * SUB + row % SUB
                    allowed = (kj < qi) | (key_at <= token)
                s, dp = products(j, PK, RK, QR)
                dq[:QR, :] += grads(j, PK, RK, QR, s, dp, allowed, sums[j])

    if final:
        rounded = (dq[...] * SCALE).astype(BF16).reshape(-1, BLOCK, HD)
        if others:
            done[...] = rounded
            last = pltpu.make_async_copy(done, dq_out.at[(place[0] + 2) % 4], sems.at[2])
            last.start()
            for copy in copies + [last]:
                copy.wait()
        else:
            dq_out[...] = rounded.reshape(dq_out.shape)


def tiles(name, unit, place, lengths, pays, keys_of, keys, sums, dq=None, final=False, others=()):
    have_sums = tuple(g is not None for g in sums)
    operands = held(*pays, *keys)
    rows = QR * len(pays)
    aliases = {}
    for n, old in enumerate(list(sums) + [dq]):
        if old is not None:
            if not others and (n < len(keys) or not final):
                aliases[2 + len(operands)] = n
            operands += held(old)
    operands += held(*others)
    dq_shape = pltpu.VMEM((rows, HD), F32)
    if final:
        dq_shape = pltpu.VMEM((len(pays), SRC, BLOCK, HD) if unit == "near" else (SRC, BLOCK, HD), BF16)
    if others:
        dq_shape = pltpu.HBM((4, SRC, BLOCK, HD), BF16)
    shapes = [pltpu.VMEM((2 * HD, KW), F32)] * len(keys) + [dq_shape]
    *sums, dq = pl.pallas_call(
        functools.partial(tiles_kernel, (unit, tuple(keys_of), have_sums, dq is not None, final, len(others))),
        in_specs=[SSPEC] * 2 + [VSPEC] * len(operands),
        out_specs=[VSPEC] * len(keys) + [ANYSPEC if others else VSPEC],
        out_shape=shapes,
        scratch_shapes=[
            pltpu.VMEM((rows, HD), BF16),
            pltpu.VMEM((rows, HD), BF16),
            pltpu.VMEM((HD, rows), BF16),
            pltpu.VMEM((HD, rows), BF16),
            pltpu.VMEM((rows, HD), F32),
            pltpu.VMEM((rows, HD), F32),
            pltpu.VMEM((rows, HD) if final else (8, HD), F32),
            pltpu.VMEM((SRC, BLOCK, HD) if others else (1, 16, HD), BF16),
            pltpu.SemaphoreType.DMA((4,)),
        ],
        input_output_aliases=aliases,
        compiler_params=pltpu.CompilerParams(vmem_limit_bytes=(18 if unit == "near" else 12) << 20),
        cost_estimate=pl.CostEstimate(flops=1, bytes_accessed=1, transcendentals=0),
        name=name,
    )(place, lengths, *operands)
    return sums, dq


def finish_kernel(parts, out):
    for b in range(SRC):
        for h in range(GROUP):
            rows = slice(h * SUB, (h + 1) * SUB)
            terms = [parts[n * SRC + b, rows, :].astype(F32) for n in range(4)]
            col = (b * GROUP + h) * HD
            out[:, col : col + HD] = (terms[0] + terms[1] + terms[2] + terms[3]).astype(BF16)


def finish(parts):
    return pl.pallas_call(
        finish_kernel,
        in_specs=[VSPEC],
        out_specs=VSPEC,
        out_shape=jax.ShapeDtypeStruct((SUB, SRC * GROUP * HD), BF16),
        name="finish",
    )(*held(parts))


def close_kernel(own, core, chip_in, dk, dv, drk, drv, chip, sem):
    load = pltpu.make_async_copy(chip_in, chip, sem)
    load.start()
    load.wait()

    def total(rows, cols):
        part = own[rows, cols] + core[rows, cols] + chip[rows, cols].astype(F32)
        return part.T

    keys, values = slice(0, HD), slice(HD, 2 * HD)
    dk[...] = total(keys, slice(0, PK)) * SCALE
    drk[...] = total(keys, slice(PK, KW)) * SCALE
    dv[...] = total(values, slice(0, PK))
    drv[...] = total(values, slice(PK, KW))


def close(own, core, chip):
    shape = lambda rows: jax.ShapeDtypeStruct((rows, HD), F32)
    return pl.pallas_call(
        close_kernel,
        in_specs=[VSPEC, VSPEC, ANYSPEC],
        out_specs=[VSPEC] * 4,
        out_shape=[shape(PK), shape(PK), shape(RK), shape(RK)],
        scratch_shapes=[pltpu.VMEM((2 * HD, KW), BF16), pltpu.SemaphoreType.DMA],
        compiler_params=pltpu.CompilerParams(vmem_limit_bytes=16 << 20),
        name="close",
    )(*held(own, core), *in_hbm([chip]))


def shift(n, s):
    return [(i, (i + s) % n) for i in range(n)]


def after(values, *earlier):
    return lax.optimization_barrier((values, earlier))[0]


def shards(
    queries,
    out_grad,
    attn_out,
    log_totals,
    prompt_keys,
    prompt_values,
    rollout_keys,
    rollout_values,
    rollout_blocks,
):
    place = jnp.stack([lax.axis_index(Y), lax.axis_index(XH), lax.axis_index(C)])
    place = place.astype(jnp.int32)
    to_next, to_last, swap = shift(4, 1), shift(4, -1), shift(2, 1)

    logs = (log_totals * LOG2E).reshape(SRC, SUB, GROUP).transpose(0, 2, 1).reshape(SRC, 1, BLOCK)
    l1 = lax.reduce_precision(logs, 8, 7)
    l2 = lax.reduce_precision(logs - l1, 8, 7)
    logs = [p.astype(BF16) for p in (l1, l2, logs - l1 - l2)]
    logs = jnp.concatenate(logs + [jnp.zeros((SRC, PAY - LROW - 3, BLOCK), BF16)], axis=1)

    payload = pack(place, queries, out_grad, attn_out)
    own = lax.all_to_all(payload, BULK, split_axis=0, concat_axis=0, tiled=True)
    kv_own = join(*after((prompt_keys, rollout_keys, prompt_values, rollout_values), payload))
    kv_c = lax.ppermute(kv_own, C, swap)
    kv_x = lax.ppermute(after(kv_own, own), XH, swap)
    own = own.at[:, LROW:PAY, :].set(logs)
    up = lax.ppermute(own, Y, to_last)
    down = lax.ppermute(own, Y, to_next)

    def run(name, pays, keys_of, keys, sums, dq=None, final=False, others=()):
        unit = name.split("_")[0]
        return tiles(name, unit, place, rollout_blocks, pays, keys_of, keys, sums, dq, final, others)

    o_own, o_core, o_chip, o_both = (0, 0), (0, 1), (1, 0), (1, 1)
    here, far = [o_own, o_core], [o_chip, o_both]
    (g_own, g_c), dq_own = run("own_here", [own], here, [kv_own, kv_c], [None, None])
    kv_x = after(kv_x, dq_own)
    kv_xc = lax.ppermute(kv_x, C, swap)
    (g_x,), dq_own = run("own_chip", [own], [o_chip], [kv_x], [None], dq_own)
    up, down = after((up, down), dq_own)
    opp = lax.ppermute(after(own, up, down), Y, shift(4, 2))
    (g_xc,), dq_own = run("own_both", [own], [o_both], [kv_xc], [None], dq_own, True)
    near = after([up, down], dq_own)
    (g_x, g_xc), dq_near = run("near_far", near, far, [kv_x, kv_xc], [g_x, g_xc])
    (g_xc,), dq_opp = run("opp_both", [opp], [o_both], [kv_xc], [g_xc])
    from_core = lax.ppermute(g_xc, C, swap)
    (g_x,), dq_opp = run("opp_chip", [opp], [o_chip], [kv_x], [g_x], dq_opp)
    to_chip = (g_x + after(from_core, dq_opp)).astype(BF16)
    from_chip = lax.ppermute(to_chip, XH, swap)
    dq_near = after(dq_near, to_chip)
    (g_own, g_c), dq_near = run(
        "near_here", near, here, [kv_own, kv_c], [g_own, g_c], dq_near, True
    )
    (g_own, g_c), dq = run(
        "opp_here", [opp], here, [kv_own, kv_c], [g_own, g_c], dq_opp, True, [dq_own, dq_near]
    )
    from_c = lax.ppermute(g_c, C, swap)
    dq, from_chip = lax.optimization_barrier((dq, from_chip))
    dq = dq.reshape(4 * SRC, BLOCK, HD)
    parts = lax.all_to_all(dq, (Y,) + BULK, split_axis=0, concat_axis=0, tiled=True)
    dk, dv, drk, drv = close(g_own, from_c, from_chip)
    query_grad = finish(after(parts, dk))
    return (query_grad, dk, dv, drk, drv)


def solution(mesh):
    fine = Mesh(mesh.devices.reshape(4, 2, 2, 4, 2), (Y, XH, C, Z, XL))
    hold, bulk = (Y, XH, C), (Z, XL)
    tokens = P(hold + bulk, None)
    split = P(hold, bulk)
    return jax.shard_map(
        shards,
        mesh=fine,
        in_specs=(tokens, tokens, tokens, split, split, split, split, split, P()),
        out_specs=(tokens, split, split, split, split),
        check_vma=False,
    )
```

profile of v0, /device:TPU:0, one launch (start us, length us, event | category | flops | bytes accessed | tf_op | source)
XLA Modules:
  0.0 109.6 jit_solution(7965080192381785932)
XLA Ops:
  0.7 2.9 %pack.1 = bf16[8,272,128]{2,1,0:T(8,128)(2,1)} custom-call(s32[3]{0:T(128)S(1)} %pad_add_fusion.place.refs_0_, bf16[16,8192]{1,0:T(8,128)(2,1)} %q_in.1, bf16[16,8192]{1,0:T(8,128)(2,1)} %g_in.1, bf16[16,8192]{1,0:T(8,128)(2,1)} %o_in.1), custom_call_target="tpu_custom_call" | custom-call | tf_op jit(solution)/shard_map/pack/pallas_call | solution.py:88
  3.6 6.3 %all-to-all-start = ((bf16[8,272,128]{2,1,0:T(8,128)(2,1)}), bf16[8,272,128]{2,1,0:T(8,128)(2,1)S(1)}, u32[]{:S(2)}, u32[]{:S(2)}) async-start(bf16[8,272,128]{2,1,0:T(8,128)(2,1)} %pack.1), calls=%async_computation | async-start | bytes 1114112 | tf_op jit(solution)/shard_map/all_to_all | solution.py:367
  10.0 1.1 join.1.refs_3_.refs_4_
  11.5 9.0 %all-to-all-done = bf16[8,272,128]{2,1,0:T(8,128)(2,1)S(1)} async-done(((bf16[8,272,128]{2,1,0:T(8,128)(2,1)}), bf16[8,272,128]{2,1,0:T(8,128)(2,1)S(1)}, u32[]{:S(2)}, u32[]{:S(2)}) %all-to-all-start) | async-done | bytes 557088 | tf_op jit(solution)/shard_map/all_to_all | solution.py:367
  20.4 2.7 %collective-permute-start.2 = (bf16[2304,128]{1,0:T(8,128)(2,1)S(1)}, bf16[2304,128]{1,0:T(8,128)(2,1)S(1)}, u32[]{:S(2)}, u32[]{:S(2)}) collective-permute-start(bf16[2304,128]{1,0:T(8,128)(2,1)S(1)} %join.1.refs_3_.refs_4_), channel_id=1, source_target_pairs={{0,16},{16,0},{1,17},{17,1},{2,18},{18,2},{3,19},{19,3},{4,20},{20... | collective-permute-start | bytes 1769480 | tf_op jit(solution)/shard_map/ppermute | solution.py:370
  23.2 1.6 %collective-permute-start.1 = (bf16[8,272,128]{2,1,0:T(8,128)(2,1)S(1)}, bf16[8,272,128]{2,1,0:T(8,128)(2,1)S(1)}, u32[]{:S(2)}, u32[]{:S(2)}) collective-permute-start(bf16[8,272,128]{2,1,0:T(8,128)(2,1)S(1)} %maximum_dynamic-update-slice_fusion.refs_2_), channel_id=1, source_target_pairs={{0,32},{32,64},{64,96},{96,0},{1,33},{33,65},{65,97},{97,1},{2,34}... | collective-permute-start | bytes 1671176 | tf_op jit(solution)/shard_map/ppermute | solution.py:373
  24.8 1.7 %collective-permute-start = (bf16[8,272,128]{2,1,0:T(8,128)(2,1)S(1)}, bf16[8,272,128]{2,1,0:T(8,128)(2,1)S(1)}, u32[]{:S(2)}, u32[]{:S(2)}) collective-permute-start(bf16[8,272,128]{2,1,0:T(8,128)(2,1)S(1)} %maximum_dynamic-update-slice_fusion.refs_2_), channel_id=1, source_target_pairs={{0,96},{32,0},{64,32},{96,64},{1,97},{33,1},{65,33},{97,65},{2,98}... | collective-permute-start | bytes 1671176 | tf_op jit(solution)/shard_map/ppermute | solution.py:372
  26.5 6.7 %own_here.1 = (f32[256,1152]{1,0:T(8,128)S(1)}, f32[256,1152]{1,0:T(8,128)S(1)}, f32[1024,128]{1,0:T(8,128)S(1)}) custom-call(s32[3]{0:T(128)S(1)} %pad_add_fusion.place.refs_0_, s32[8]{0:T(128)S(1)} %copy-done, bf16[8,272,128]{2,1,0:T(8,128)(2,1)S(1)} %maximum_dynamic-update-slice_fusion.refs_2_, bf16[2304,128]{1,0:T(8,128)(2,1)S(1)} %join.1.refs_3_.refs_4_, ...), custom_call_target="tpu_custom_call" | custom-call | flops 1 | bytes 1 | tf_op jit(solution)/shard_map/own_here/pallas_call | solution.py:265
  33.2 2.6 %collective-permute-done.2.refs_3_.refs_4_ = bf16[2304,128]{1,0:T(8,128)(2,1)S(1)} collective-permute-done((bf16[2304,128]{1,0:T(8,128)(2,1)S(1)}, bf16[2304,128]{1,0:T(8,128)(2,1)S(1)}, u32[]{:S(2)}, u32[]{:S(2)}) %collective-permute-start.2) | collective-permute-done | bytes 589856 | tf_op jit(solution)/shard_map/ppermute | solution.py:370
  35.8 3.1 %own_chip.1 = (f32[256,1152]{1,0:T(8,128)S(1)}, f32[1024,128]{1,0:T(8,128)S(1)}) custom-call(s32[3]{0:T(128)S(1)} %pad_add_fusion.place.refs_0_, s32[8]{0:T(128)S(1)} %copy-done, bf16[8,272,128]{2,1,0:T(8,128)(2,1)S(1)} %maximum_dynamic-update-slice_fusion.refs_2_, ...), custom_call_target="tpu_custom_call", output_to_operand_aliasing={{1}: (4, {})} | custom-call | flops 1 | bytes 1 | tf_op jit(solution)/shard_map/own_chip/pallas_call | solution.py:265
  38.9 3.5 %collective-permute-start.4 = (bf16[8,272,128]{2,1,0:T(8,128)(2,1)S(1)}, bf16[8,272,128]{2,1,0:T(8,128)(2,1)S(1)}, u32[]{:S(2)}, u32[]{:S(2)}) collective-permute-start(bf16[8,272,128]{2,1,0:T(8,128)(2,1)S(1)} %maximum_dynamic-update-slice_fusion.refs_2_), channel_id=1, source_target_pairs={{0,64},{32,96},{64,0},{96,32},{1,65},{33,97},{65,1},{97,33},{2,66}... | collective-permute-start | bytes 1671176 | tf_op jit(solution)/shard_map/ppermute | solution.py:386
  42.4 3.1 %own_both.1 = (f32[256,1152]{1,0:T(8,128)S(1)}, bf16[8,128,128]{2,1,0:T(8,128)(2,1)S(1)}) custom-call(s32[3]{0:T(128)S(1)} %pad_add_fusion.place.refs_0_, s32[8]{0:T(128)S(1)} %copy-done, bf16[8,272,128]{2,1,0:T(8,128)(2,1)S(1)} %maximum_dynamic-update-slice_fusion.refs_2_, bf16[2304,128]{1,0:T(8,128)(2,1)S(1)} %collective-permute-done.5.refs_3_.refs_5_, ...), custom_call_target="tpu_custom_call" | custom-call | flops 1 | bytes 1 | tf_op jit(solution)/shard_map/own_both/pallas_call | solution.py:265
  45.5 11.1 %near_far.1 = (f32[256,1152]{1,0:T(8,128)S(1)}, f32[256,1152]{1,0:T(8,128)S(1)}, f32[2048,128]{1,0:T(8,128)S(1)}) custom-call(s32[3]{0:T(128)S(1)} %pad_add_fusion.place.refs_0_, s32[8]{0:T(128)S(1)} %copy-done, bf16[8,272,128]{2,1,0:T(8,128)(2,1)S(1)} %collective-permute-done.refs_2_, ...), custom_call_target="tpu_custom_call", output_to_operand_aliasing={{0}: (6, {}), {1}: (7, {})} | custom-call | flops 1 | bytes 1 | tf_op jit(solution)/shard_map/near_far/pallas_call | solution.py:265
  56.6 3.1 %opp_both.1 = (f32[256,1152]{1,0:T(8,128)S(1)}, f32[1024,128]{1,0:T(8,128)S(1)}) custom-call(s32[3]{0:T(128)S(1)} %pad_add_fusion.place.refs_0_, s32[8]{0:T(128)S(1)} %copy-done, bf16[8,272,128]{2,1,0:T(8,128)(2,1)S(1)} %collective-permute-done.4.refs_2_, ...), custom_call_target="tpu_custom_call", output_to_operand_aliasing={{0}: (4, {})} | custom-call | flops 1 | bytes 1 | tf_op jit(solution)/shard_map/opp_both/pallas_call | solution.py:265
  59.7 0.3 collective-permute-start.6
  60.0 3.1 %opp_chip.1 = (f32[256,1152]{1,0:T(8,128)S(1)}, f32[1024,128]{1,0:T(8,128)S(1)}) custom-call(s32[3]{0:T(128)S(1)} %pad_add_fusion.place.refs_0_, s32[8]{0:T(128)S(1)} %copy-done, bf16[8,272,128]{2,1,0:T(8,128)(2,1)S(1)} %collective-permute-done.4.refs_2_, ...), custom_call_target="tpu_custom_call", output_to_operand_aliasing={{0}: (4, {}), {1}: (5, {})} | custom-call | flops 1 | bytes 1 | tf_op jit(solution)/shard_map/opp_chip/pallas_call | solution.py:265
  63.1 0.1 add_convert_fusion
  63.2 3.6 %collective-permute-start.7 = (bf16[256,1152]{1,0:T(8,128)(2,1)S(1)}, bf16[256,1152]{1,0:T(8,128)(2,1)S(1)}, u32[]{:S(2)}, u32[]{:S(2)}) collective-permute-start(bf16[256,1152]{1,0:T(8,128)(2,1)S(1)} %add_convert_fusion), channel_id=1, source_target_pairs={{0,16},{16,0},{1,17},{17,1},{2,18},{18,2},{3,19},{19,3},{4,20},{20... | collective-permute-start | bytes 1769480 | tf_op jit(solution)/shard_map/ppermute | solution.py:394
  66.8 11.1 %near_here.1 = (f32[256,1152]{1,0:T(8,128)S(1)}, f32[256,1152]{1,0:T(8,128)S(1)}, bf16[2,8,128,128]{3,2,1,0:T(8,128)(2,1)S(1)}) custom-call(s32[3]{0:T(128)S(1)} %pad_add_fusion.place.refs_0_, s32[8]{0:T(128)S(1)} %copy-done, bf16[8,272,128]{2,1,0:T(8,128)(2,1)S(1)} %collective-permute-done.refs_2_, ...), custom_call_target="tpu_custom_call", output_to_operand_aliasing={{0}: (6, {}), {1}: (7, {})} | custom-call | flops 1 | bytes 1 | tf_op jit(solution)/shard_map/near_here/pallas_call | solution.py:265
  77.9 7.7 %opp_here.1 = (f32[256,1152]{1,0:T(8,128)S(1)}, f32[256,1152]{1,0:T(8,128)}, bf16[4,8,128,128]{3,2,1,0:T(8,128)(2,1)}) custom-call(s32[3]{0:T(128)S(1)} %pad_add_fusion.place.refs_0_, s32[8]{0:T(128)S(1)} %copy-done, bf16[8,272,128]{2,1,0:T(8,128)(2,1)S(1)} %collective-permute-done.4.refs_2_, bf16[2304,128]{1,0:T(8,128)(2,1)S(1)} %join.1.refs_3_.refs_4_, ...), custom_call_target="tpu_custom_call" | custom-call | flops 1 | bytes 1 | tf_op jit(solution)/shard_map/opp_here/pallas_call | solution.py:265
  85.7 4.1 %all-to-all-start.1 = ((bf16[32,128,128]{2,1,0:T(8,128)(2,1)}), bf16[32,128,128]{2,1,0:T(8,128)(2,1)S(1)}, u32[]{:S(2)}, u32[]{:S(2)}) async-start(bf16[32,128,128]{2,1,0:T(8,128)(2,1)} %bitcast.9), calls=%async_computation.1 | async-start | bytes 2097152 | tf_op jit(solution)/shard_map/all_to_all | solution.py:405
  89.8 3.7 %close.1 = (f32[1024,128]{1,0:T(8,128)}, f32[1024,128]{1,0:T(8,128)}, f32[128,128]{1,0:T(8,128)}, f32[128,128]{1,0:T(8,128)}) custom-call(f32[256,1152]{1,0:T(8,128)S(1)} %get-tuple-element.89.own, f32[256,1152]{1,0:T(8,128)} %collective-permute-done.8.core, bf16[256,1152]{1,0:T(8,128)(2,1)} %copy-done.1), custom_call_target="tpu_custom_call" | custom-call | tf_op jit(solution)/shard_map/close/pallas_call | solution.py:326
  93.5 15.3 %all-to-all-done.1.parts = bf16[32,128,128]{2,1,0:T(8,128)(2,1)S(1)} async-done(((bf16[32,128,128]{2,1,0:T(8,128)(2,1)}), bf16[32,128,128]{2,1,0:T(8,128)(2,1)S(1)}, u32[]{:S(2)}, u32[]{:S(2)}) %all-to-all-start.1) | async-done | bytes 1048608 | tf_op jit(solution)/shard_map/all_to_all | solution.py:405
  108.8 0.8 finish.1
  (26 shorter events, 0.6 us)
Async XLA Ops:
  3.6 7.5 %copy-start.2 = (f32[128,8]{0,1:T(8,128)S(1)}, f32[128,8]{0,1:T(8,128)}, u32[]{:S(2)}) copy-start(f32[128,8]{0,1:T(8,128)} %param.14) | copy-start | bytes 12292
  3.6 22.9 %copy-start = (s32[8]{0:T(128)S(1)}, s32[8]{0:T(128)}, u32[]{:S(2)}) copy-start(s32[8]{0:T(128)} %refs_1_.15) | copy-start | bytes 100
  3.6 16.8 %all-to-all-start = ((bf16[8,272,128]{2,1,0:T(8,128)(2,1)}), bf16[8,272,128]{2,1,0:T(8,128)(2,1)S(1)}, u32[]{:S(2)}, u32[]{:S(2)}) async-start(bf16[8,272,128]{2,1,0:T(8,128)(2,1)} %pack.1), calls=%async_computation | async-start | bytes 1114112 | tf_op jit(solution)/shard_map/all_to_all | solution.py:367
  11.1 15.4 %collective-permute-start.3 = (bf16[2304,128]{1,0:T(8,128)(2,1)S(1)}, bf16[2304,128]{1,0:T(8,128)(2,1)S(1)}, u32[]{:S(2)}, u32[]{:S(2)}) collective-permute-start(bf16[2304,128]{1,0:T(8,128)(2,1)S(1)} %join.1.refs_3_.refs_4_), channel_id=1, source_target_pairs={{0,8},{8,0},{1,9},{9,1},{2,10},{10,2},{3,11},{11,3},{4,12},{12,4},... | collective-permute-start | bytes 1769480 | tf_op jit(solution)/shard_map/ppermute | solution.py:369
  20.4 15.4 %collective-permute-start.2 = (bf16[2304,128]{1,0:T(8,128)(2,1)S(1)}, bf16[2304,128]{1,0:T(8,128)(2,1)S(1)}, u32[]{:S(2)}, u32[]{:S(2)}) collective-permute-start(bf16[2304,128]{1,0:T(8,128)(2,1)S(1)} %join.1.refs_3_.refs_4_), channel_id=1, source_target_pairs={{0,16},{16,0},{1,17},{17,1},{2,18},{18,2},{3,19},{19,3},{4,20},{20... | collective-permute-start | bytes 1769480 | tf_op jit(solution)/shard_map/ppermute | solution.py:370
  23.2 15.7 %collective-permute-start.1 = (bf16[8,272,128]{2,1,0:T(8,128)(2,1)S(1)}, bf16[8,272,128]{2,1,0:T(8,128)(2,1)S(1)}, u32[]{:S(2)}, u32[]{:S(2)}) collective-permute-start(bf16[8,272,128]{2,1,0:T(8,128)(2,1)S(1)} %maximum_dynamic-update-slice_fusion.refs_2_), channel_id=1, source_target_pairs={{0,32},{32,64},{64,96},{96,0},{1,33},{33,65},{65,97},{97,1},{2,34}... | collective-permute-start | bytes 1671176 | tf_op jit(solution)/shard_map/ppermute | solution.py:373
  24.8 14.1 %collective-permute-start = (bf16[8,272,128]{2,1,0:T(8,128)(2,1)S(1)}, bf16[8,272,128]{2,1,0:T(8,128)(2,1)S(1)}, u32[]{:S(2)}, u32[]{:S(2)}) collective-permute-start(bf16[8,272,128]{2,1,0:T(8,128)(2,1)S(1)} %maximum_dynamic-update-slice_fusion.refs_2_), channel_id=1, source_target_pairs={{0,96},{32,0},{64,32},{96,64},{1,97},{33,1},{65,33},{97,65},{2,98}... | collective-permute-start | bytes 1671176 | tf_op jit(solution)/shard_map/ppermute | solution.py:372
  35.8 6.6 %collective-permute-start.5 = (bf16[2304,128]{1,0:T(8,128)(2,1)S(1)}, bf16[2304,128]{1,0:T(8,128)(2,1)S(1)}, u32[]{:S(2)}, u32[]{:S(2)}) collective-permute-start(bf16[2304,128]{1,0:T(8,128)(2,1)S(1)} %collective-permute-done.2.refs_3_.refs_4_), channel_id=1, source_target_pairs={{0,8},{8,0},{1,9},{9,1},{2,10},{10,2},{3,11},{11,3},{4,12},{12,4},... | collective-permute-start | bytes 1769480 | tf_op jit(solution)/shard_map/ppermute | solution.py:383
  38.9 17.7 %collective-permute-start.4 = (bf16[8,272,128]{2,1,0:T(8,128)(2,1)S(1)}, bf16[8,272,128]{2,1,0:T(8,128)(2,1)S(1)}, u32[]{:S(2)}, u32[]{:S(2)}) collective-permute-start(bf16[8,272,128]{2,1,0:T(8,128)(2,1)S(1)} %maximum_dynamic-update-slice_fusion.refs_2_), channel_id=1, source_target_pairs={{0,64},{32,96},{64,0},{96,32},{1,65},{33,97},{65,1},{97,33},{2,66}... | collective-permute-start | bytes 1671176 | tf_op jit(solution)/shard_map/ppermute | solution.py:386
  59.7 3.4 %collective-permute-start.6 = (f32[256,1152]{1,0:T(8,128)S(1)}, f32[256,1152]{1,0:T(8,128)S(1)}, u32[]{:S(2)}, u32[]{:S(2)}) collective-permute-start(f32[256,1152]{1,0:T(8,128)S(1)} %get-tuple-element.80), channel_id=1, source_target_pairs={{0,8},{8,0},{1,9},{9,1},{2,10},{10,2},{3,11},{11,3},{4,12},{12,4},... | collective-permute-start | bytes 3538952 | tf_op jit(solution)/shard_map/ppermute | solution.py:391
  63.2 22.5 %collective-permute-start.7 = (bf16[256,1152]{1,0:T(8,128)(2,1)S(1)}, bf16[256,1152]{1,0:T(8,128)(2,1)S(1)}, u32[]{:S(2)}, u32[]{:S(2)}) collective-permute-start(bf16[256,1152]{1,0:T(8,128)(2,1)S(1)} %add_convert_fusion), channel_id=1, source_target_pairs={{0,16},{16,0},{1,17},{17,1},{2,18},{18,2},{3,19},{19,3},{4,20},{20... | collective-permute-start | bytes 1769480 | tf_op jit(solution)/shard_map/ppermute | solution.py:394
  85.6 4.2 %collective-permute-start.8 = (f32[256,1152]{1,0:T(8,128)}, f32[256,1152]{1,0:T(8,128)}, u32[]{:S(2)}, u32[]{:S(2)}) collective-permute-start(f32[256,1152]{1,0:T(8,128)} %get-tuple-element.90), channel_id=1, source_target_pairs={{0,8},{8,0},{1,9},{9,1},{2,10},{10,2},{3,11},{11,3},{4,12},{12,4},... | collective-permute-start | bytes 3538952 | tf_op jit(solution)/shard_map/ppermute | solution.py:402
  85.7 4.1 %copy-start.1 = (bf16[256,1152]{1,0:T(8,128)(2,1)}, bf16[256,1152]{1,0:T(8,128)(2,1)S(1)}, u32[]{:S(2)}) copy-start(bf16[256,1152]{1,0:T(8,128)(2,1)S(1)} %collective-permute-done.7.chip_in) | copy-start | bytes 1769476
  85.7 23.1 %all-to-all-start.1 = ((bf16[32,128,128]{2,1,0:T(8,128)(2,1)}), bf16[32,128,128]{2,1,0:T(8,128)(2,1)S(1)}, u32[]{:S(2)}, u32[]{:S(2)}) async-start(bf16[32,128,128]{2,1,0:T(8,128)(2,1)} %bitcast.9), calls=%async_computation.1 | async-start | bytes 2097152 | tf_op jit(solution)/shard_map/all_to_all | solution.py:405
where the time goes:
time: 110 us
  Pallas kernels  57.4 us (52%)
  waiting for transfers between devices  26.9 us (24%)
  starting transfers between devices  23.9 us (22%)
    pallas_call x8, Pallas kernels, tiles(): pl.pallas_call(functools.partial(tiles_kernel, (unit, tuple(keys_of), hav...  48.9 us
    all_to_all x1, waiting for transfers between devices, shards(): lax.all_to_all(dq, (Y,) + BULK, split_axis=0, concat_axis=0, tiled=True)  15.3 us
    all_to_all x1, waiting for transfers between devices, shards(): own = lax.all_to_all(payload, BULK, split_axis=0, concat_axis=0, tiled=True)  8.95 us
    all_to_all x1, starting transfers between devices, shards(): own = lax.all_to_all(payload, BULK, split_axis=0, concat_axis=0, tiled=True)  6.34 us
    all_to_all x1, starting transfers between devices, shards(): lax.all_to_all(dq, (Y,) + BULK, split_axis=0, concat_axis=0, tiled=True)  4.09 us
    pallas_call x1, Pallas kernels, close(): pl.pallas_call(close_kernel, in_specs=[VSPEC, VSPEC, ANYSPEC], out_specs=...  3.68 us
    ppermute x1, starting transfers between devices, shards(): from_chip = lax.ppermute(to_chip, XH, swap)  3.57 us
    ppermute x1, starting transfers between devices, shards(): opp = lax.ppermute(after(own, up, down), Y, shift(4, 2))  3.46 us
  transfers between devices with their start and end apart: 11, of which 3 were waited for; matrix products, arithmetic and copies ran while one was open for 0% of the time, Pallas kernels for 46%

commit v1 on v0

--- a/solution.py
+++ b/solution.py
@@ -367,7 +367,7 @@
     own = lax.all_to_all(payload, BULK, split_axis=0, concat_axis=0, tiled=True)
     kv_own = join(*after((prompt_keys, rollout_keys, prompt_values, rollout_values), payload))
     kv_c = lax.ppermute(kv_own, C, swap)
-    kv_x = lax.ppermute(after(kv_own, own), XH, swap)
+    kv_x = lax.ppermute(kv_own, XH, swap)
     own = own.at[:, LROW:PAY, :].set(logs)
     up = lax.ppermute(own, Y, to_last)
     down = lax.ppermute(own, Y, to_next)

time: 110 us -> 106 us (0.964)
  waiting for transfers between devices: 26.9 us -> 22.3 us
  starting transfers between devices: 23.9 us -> 25 us
    ppermute x1, waiting for transfers between devices: 2.62 us -> 0.04 us  [shards(): kv_x = lax.ppermute(kv_own, XH, swap)]
    all_to_all x1, starting transfers between devices: 4.09 us -> 5.76 us  [shards(): lax.all_to_all(dq, (Y,) + BULK, split_axis=0, concat_axis=0, tiled=True)]
    all_to_all x1, waiting for transfers between devices: 8.95 us -> 7.62 us  [shards(): own = lax.all_to_all(payload, BULK, split_axis=0, concat_axis=0, tiled=True)]
  transfers between devices with their start and end apart: 11 -> 11, of which waited for: 3 -> 2; matrix products, arithmetic and copies ran while one was open for 0% -> 0% of each run, Pallas kernels for 46% -> 48%
where the time goes in v1:
time: 106 us
  Pallas kernels  57.4 us (54%)
  starting transfers between devices  25 us (24%)
  waiting for transfers between devices  22.3 us (21%)
    pallas_call x8, Pallas kernels, tiles(): pl.pallas_call(functools.partial(tiles_kernel, (unit, tuple(keys_of), hav...  48.9 us
    all_to_all x1, waiting for transfers between devices, shards(): lax.all_to_all(dq, (Y,) + BULK, split_axis=0, concat_axis=0, tiled=True)  14.6 us
    all_to_all x1, waiting for transfers between devices, shards(): own = lax.all_to_all(payload, BULK, split_axis=0, concat_axis=0, tiled=True)  7.62 us
    all_to_all x1, starting transfers between devices, shards(): own = lax.all_to_all(payload, BULK, split_axis=0, concat_axis=0, tiled=True)  6.34 us
    all_to_all x1, starting transfers between devices, shards(): lax.all_to_all(dq, (Y,) + BULK, split_axis=0, concat_axis=0, tiled=True)  5.76 us
    pallas_call x1, Pallas kernels, close(): pl.pallas_call(close_kernel, in_specs=[VSPEC, VSPEC, ANYSPEC], out_specs=...  3.68 us
    ppermute x1, starting transfers between devices, shards(): opp = lax.ppermute(after(own, up, down), Y, shift(4, 2))  3.39 us
    pallas_call x1, Pallas kernels, pack(): pl.pallas_call(pack_kernel, in_specs=[SSPEC] + [ANYSPEC] * 3, out_specs=V...  2.9 us
  transfers between devices with their start and end apart: 11, of which 2 were waited for; matrix products, arithmetic and copies ran while one was open for 0% of the time, Pallas kernels for 48%

profile of v1, /device:TPU:0, one launch (start us, length us, event | category | flops | bytes accessed | tf_op | source)
XLA Modules:
  0.0 106.1 jit_solution(7843867353119476365)
XLA Ops:
  0.7 2.9 %pack.1 = bf16[8,272,128]{2,1,0:T(8,128)(2,1)} custom-call(s32[3]{0:T(128)S(1)} %pad_add_fusion.place.refs_0_, bf16[16,8192]{1,0:T(8,128)(2,1)} %q_in.1, bf16[16,8192]{1,0:T(8,128)(2,1)} %g_in.1, bf16[16,8192]{1,0:T(8,128)(2,1)} %o_in.1), custom_call_target="tpu_custom_call" | custom-call | tf_op jit(solution)/shard_map/pack/pallas_call | solution.py:88
  3.6 6.3 %all-to-all-start = ((bf16[8,272,128]{2,1,0:T(8,128)(2,1)}), bf16[8,272,128]{2,1,0:T(8,128)(2,1)S(1)}, u32[]{:S(2)}, u32[]{:S(2)}) async-start(bf16[8,272,128]{2,1,0:T(8,128)(2,1)} %pack.1), calls=%async_computation | async-start | bytes 1114112 | tf_op jit(solution)/shard_map/all_to_all | solution.py:367
  10.0 1.1 %join.1.refs_3_.refs_4_ = bf16[2304,128]{1,0:T(8,128)(2,1)S(1)} custom-call(bf16[1024,128]{1,0:T(8,128)(2,1)} %pk, bf16[128,128]{1,0:T(8,128)(2,1)} %rk, bf16[1024,128]{1,0:T(8,128)(2,1)} %pv, bf16[128,128]{1,0:T(8,128)(2,1)} %rv), custom_call_target="tpu_custom_call" | custom-call | tf_op jit(solution)/shard_map/join/pallas_call | solution.py:112
  11.2 2.8 %collective-permute-start.2 = (bf16[2304,128]{1,0:T(8,128)(2,1)S(1)}, bf16[2304,128]{1,0:T(8,128)(2,1)S(1)}, u32[]{:S(2)}, u32[]{:S(2)}) collective-permute-start(bf16[2304,128]{1,0:T(8,128)(2,1)S(1)} %join.1.refs_3_.refs_4_), channel_id=1, source_target_pairs={{0,16},{16,0},{1,17},{17,1},{2,18},{18,2},{3,19},{19,3},{4,20},{20... | collective-permute-start | bytes 1769480 | tf_op jit(solution)/shard_map/ppermute | solution.py:370
  14.3 7.6 %all-to-all-done = bf16[8,272,128]{2,1,0:T(8,128)(2,1)S(1)} async-done(((bf16[8,272,128]{2,1,0:T(8,128)(2,1)}), bf16[8,272,128]{2,1,0:T(8,128)(2,1)S(1)}, u32[]{:S(2)}, u32[]{:S(2)}) %all-to-all-start) | async-done | bytes 557088 | tf_op jit(solution)/shard_map/all_to_all | solution.py:367
  22.0 1.6 %collective-permute-start.1 = (bf16[8,272,128]{2,1,0:T(8,128)(2,1)S(1)}, bf16[8,272,128]{2,1,0:T(8,128)(2,1)S(1)}, u32[]{:S(2)}, u32[]{:S(2)}) collective-permute-start(bf16[8,272,128]{2,1,0:T(8,128)(2,1)S(1)} %maximum_dynamic-update-slice_fusion.refs_2_), channel_id=1, source_target_pairs={{0,32},{32,64},{64,96},{96,0},{1,33},{33,65},{65,97},{97,1},{2,34}... | collective-permute-start | bytes 1671176 | tf_op jit(solution)/shard_map/ppermute | solution.py:373
  23.6 1.7 %collective-permute-start = (bf16[8,272,128]{2,1,0:T(8,128)(2,1)S(1)}, bf16[8,272,128]{2,1,0:T(8,128)(2,1)S(1)}, u32[]{:S(2)}, u32[]{:S(2)}) collective-permute-start(bf16[8,272,128]{2,1,0:T(8,128)(2,1)S(1)} %maximum_dynamic-update-slice_fusion.refs_2_), channel_id=1, source_target_pairs={{0,96},{32,0},{64,32},{96,64},{1,97},{33,1},{65,33},{97,65},{2,98}... | collective-permute-start | bytes 1671176 | tf_op jit(solution)/shard_map/ppermute | solution.py:372
  25.2 6.7 %own_here.1 = (f32[256,1152]{1,0:T(8,128)S(1)}, f32[256,1152]{1,0:T(8,128)S(1)}, f32[1024,128]{1,0:T(8,128)S(1)}) custom-call(s32[3]{0:T(128)S(1)} %pad_add_fusion.place.refs_0_, s32[8]{0:T(128)S(1)} %copy-done, bf16[8,272,128]{2,1,0:T(8,128)(2,1)S(1)} %maximum_dynamic-update-slice_fusion.refs_2_, bf16[2304,128]{1,0:T(8,128)(2,1)S(1)} %join.1.refs_3_.refs_4_, ...), custom_call_target="tpu_custom_call" | custom-call | flops 1 | bytes 1 | tf_op jit(solution)/shard_map/own_here/pallas_call | solution.py:265
  32.0 3.1 %own_chip.1 = (f32[256,1152]{1,0:T(8,128)S(1)}, f32[1024,128]{1,0:T(8,128)S(1)}) custom-call(s32[3]{0:T(128)S(1)} %pad_add_fusion.place.refs_0_, s32[8]{0:T(128)S(1)} %copy-done, bf16[8,272,128]{2,1,0:T(8,128)(2,1)S(1)} %maximum_dynamic-update-slice_fusion.refs_2_, ...), custom_call_target="tpu_custom_call", output_to_operand_aliasing={{1}: (4, {})} | custom-call | flops 1 | bytes 1 | tf_op jit(solution)/shard_map/own_chip/pallas_call | solution.py:265
  35.1 3.4 %collective-permute-start.4 = (bf16[8,272,128]{2,1,0:T(8,128)(2,1)S(1)}, bf16[8,272,128]{2,1,0:T(8,128)(2,1)S(1)}, u32[]{:S(2)}, u32[]{:S(2)}) collective-permute-start(bf16[8,272,128]{2,1,0:T(8,128)(2,1)S(1)} %maximum_dynamic-update-slice_fusion.refs_2_), channel_id=1, source_target_pairs={{0,64},{32,96},{64,0},{96,32},{1,65},{33,97},{65,1},{97,33},{2,66}... | collective-permute-start | bytes 1671176 | tf_op jit(solution)/shard_map/ppermute | solution.py:386
  38.5 3.1 %own_both.1 = (f32[256,1152]{1,0:T(8,128)S(1)}, bf16[8,128,128]{2,1,0:T(8,128)(2,1)S(1)}) custom-call(s32[3]{0:T(128)S(1)} %pad_add_fusion.place.refs_0_, s32[8]{0:T(128)S(1)} %copy-done, bf16[8,272,128]{2,1,0:T(8,128)(2,1)S(1)} %maximum_dynamic-update-slice_fusion.refs_2_, bf16[2304,128]{1,0:T(8,128)(2,1)S(1)} %collective-permute-done.5.refs_3_.refs_5_, ...), custom_call_target="tpu_custom_call" | custom-call | flops 1 | bytes 1 | tf_op jit(solution)/shard_map/own_both/pallas_call | solution.py:265
  41.6 11.1 %near_far.1 = (f32[256,1152]{1,0:T(8,128)S(1)}, f32[256,1152]{1,0:T(8,128)S(1)}, f32[2048,128]{1,0:T(8,128)S(1)}) custom-call(s32[3]{0:T(128)S(1)} %pad_add_fusion.place.refs_0_, s32[8]{0:T(128)S(1)} %copy-done, bf16[8,272,128]{2,1,0:T(8,128)(2,1)S(1)} %collective-permute-done.refs_2_, ...), custom_call_target="tpu_custom_call", output_to_operand_aliasing={{0}: (6, {}), {1}: (7, {})} | custom-call | flops 1 | bytes 1 | tf_op jit(solution)/shard_map/near_far/pallas_call | solution.py:265
  52.7 3.1 %opp_both.1 = (f32[256,1152]{1,0:T(8,128)S(1)}, f32[1024,128]{1,0:T(8,128)S(1)}) custom-call(s32[3]{0:T(128)S(1)} %pad_add_fusion.place.refs_0_, s32[8]{0:T(128)S(1)} %copy-done, bf16[8,272,128]{2,1,0:T(8,128)(2,1)S(1)} %collective-permute-done.4.refs_2_, ...), custom_call_target="tpu_custom_call", output_to_operand_aliasing={{0}: (4, {})} | custom-call | flops 1 | bytes 1 | tf_op jit(solution)/shard_map/opp_both/pallas_call | solution.py:265
  55.8 0.3 collective-permute-start.6
  56.1 3.1 %opp_chip.1 = (f32[256,1152]{1,0:T(8,128)S(1)}, f32[1024,128]{1,0:T(8,128)S(1)}) custom-call(s32[3]{0:T(128)S(1)} %pad_add_fusion.place.refs_0_, s32[8]{0:T(128)S(1)} %copy-done, bf16[8,272,128]{2,1,0:T(8,128)(2,1)S(1)} %collective-permute-done.4.refs_2_, ...), custom_call_target="tpu_custom_call", output_to_operand_aliasing={{0}: (4, {}), {1}: (5, {})} | custom-call | flops 1 | bytes 1 | tf_op jit(solution)/shard_map/opp_chip/pallas_call | solution.py:265
  59.2 0.1 add_convert_fusion
  59.3 2.7 %collective-permute-start.7 = (bf16[256,1152]{1,0:T(8,128)(2,1)S(1)}, bf16[256,1152]{1,0:T(8,128)(2,1)S(1)}, u32[]{:S(2)}, u32[]{:S(2)}) collective-permute-start(bf16[256,1152]{1,0:T(8,128)(2,1)S(1)} %add_convert_fusion), channel_id=1, source_target_pairs={{0,16},{16,0},{1,17},{17,1},{2,18},{18,2},{3,19},{19,3},{4,20},{20... | collective-permute-start | bytes 1769480 | tf_op jit(solution)/shard_map/ppermute | solution.py:394
  62.1 11.1 %near_here.1 = (f32[256,1152]{1,0:T(8,128)S(1)}, f32[256,1152]{1,0:T(8,128)S(1)}, bf16[2,8,128,128]{3,2,1,0:T(8,128)(2,1)S(1)}) custom-call(s32[3]{0:T(128)S(1)} %pad_add_fusion.place.refs_0_, s32[8]{0:T(128)S(1)} %copy-done, bf16[8,272,128]{2,1,0:T(8,128)(2,1)S(1)} %collective-permute-done.refs_2_, ...), custom_call_target="tpu_custom_call", output_to_operand_aliasing={{0}: (6, {}), {1}: (7, {})} | custom-call | flops 1 | bytes 1 | tf_op jit(solution)/shard_map/near_here/pallas_call | solution.py:265
  73.2 7.7 %opp_here.1 = (f32[256,1152]{1,0:T(8,128)S(1)}, f32[256,1152]{1,0:T(8,128)}, bf16[4,8,128,128]{3,2,1,0:T(8,128)(2,1)}) custom-call(s32[3]{0:T(128)S(1)} %pad_add_fusion.place.refs_0_, s32[8]{0:T(128)S(1)} %copy-done, bf16[8,272,128]{2,1,0:T(8,128)(2,1)S(1)} %collective-permute-done.4.refs_2_, bf16[2304,128]{1,0:T(8,128)(2,1)S(1)} %join.1.refs_3_.refs_4_, ...), custom_call_target="tpu_custom_call" | custom-call | flops 1 | bytes 1 | tf_op jit(solution)/shard_map/opp_here/pallas_call | solution.py:265
  80.9 0.3 collective-permute-start.8
  81.2 5.8 %all-to-all-start.1 = ((bf16[32,128,128]{2,1,0:T(8,128)(2,1)}), bf16[32,128,128]{2,1,0:T(8,128)(2,1)S(1)}, u32[]{:S(2)}, u32[]{:S(2)}) async-start(bf16[32,128,128]{2,1,0:T(8,128)(2,1)} %bitcast.9), calls=%async_computation.1 | async-start | bytes 2097152 | tf_op jit(solution)/shard_map/all_to_all | solution.py:405
  87.0 3.7 %close.1 = (f32[1024,128]{1,0:T(8,128)}, f32[1024,128]{1,0:T(8,128)}, f32[128,128]{1,0:T(8,128)}, f32[128,128]{1,0:T(8,128)}) custom-call(f32[256,1152]{1,0:T(8,128)S(1)} %get-tuple-element.87.own, f32[256,1152]{1,0:T(8,128)} %collective-permute-done.8.core, bf16[256,1152]{1,0:T(8,128)(2,1)} %copy-done.1), custom_call_target="tpu_custom_call" | custom-call | tf_op jit(solution)/shard_map/close/pallas_call | solution.py:326
  90.7 14.6 %all-to-all-done.1.parts = bf16[32,128,128]{2,1,0:T(8,128)(2,1)S(1)} async-done(((bf16[32,128,128]{2,1,0:T(8,128)(2,1)}), bf16[32,128,128]{2,1,0:T(8,128)(2,1)S(1)}, u32[]{:S(2)}, u32[]{:S(2)}) %all-to-all-start.1) | async-done | bytes 1048608 | tf_op jit(solution)/shard_map/all_to_all | solution.py:405
  105.3 0.8 finish.1
  (26 shorter events, 0.6 us)
Async XLA Ops:
  3.6 10.4 %copy-start.2 = (f32[128,8]{0,1:T(8,128)S(1)}, f32[128,8]{0,1:T(8,128)}, u32[]{:S(2)}) copy-start(f32[128,8]{0,1:T(8,128)} %param.14) | copy-start | bytes 12292
  3.6 21.6 %copy-start = (s32[8]{0:T(128)S(1)}, s32[8]{0:T(128)}, u32[]{:S(2)}) copy-start(s32[8]{0:T(128)} %refs_1_.15) | copy-start | bytes 100
  3.6 18.2 %all-to-all-start = ((bf16[8,272,128]{2,1,0:T(8,128)(2,1)}), bf16[8,272,128]{2,1,0:T(8,128)(2,1)S(1)}, u32[]{:S(2)}, u32[]{:S(2)}) async-start(bf16[8,272,128]{2,1,0:T(8,128)(2,1)} %pack.1), calls=%async_computation | async-start | bytes 1114112 | tf_op jit(solution)/shard_map/all_to_all | solution.py:367
  11.1 14.2 %collective-permute-start.3 = (bf16[2304,128]{1,0:T(8,128)(2,1)S(1)}, bf16[2304,128]{1,0:T(8,128)(2,1)S(1)}, u32[]{:S(2)}, u32[]{:S(2)}) collective-permute-start(bf16[2304,128]{1,0:T(8,128)(2,1)S(1)} %join.1.refs_3_.refs_4_), channel_id=1, source_target_pairs={{0,8},{8,0},{1,9},{9,1},{2,10},{10,2},{3,11},{11,3},{4,12},{12,4},... | collective-permute-start | bytes 1769480 | tf_op jit(solution)/shard_map/ppermute | solution.py:369
  11.2 20.8 %collective-permute-start.2 = (bf16[2304,128]{1,0:T(8,128)(2,1)S(1)}, bf16[2304,128]{1,0:T(8,128)(2,1)S(1)}, u32[]{:S(2)}, u32[]{:S(2)}) collective-permute-start(bf16[2304,128]{1,0:T(8,128)(2,1)S(1)} %join.1.refs_3_.refs_4_), channel_id=1, source_target_pairs={{0,16},{16,0},{1,17},{17,1},{2,18},{18,2},{3,19},{19,3},{4,20},{20... | collective-permute-start | bytes 1769480 | tf_op jit(solution)/shard_map/ppermute | solution.py:370
  22.0 13.1 %collective-permute-start.1 = (bf16[8,272,128]{2,1,0:T(8,128)(2,1)S(1)}, bf16[8,272,128]{2,1,0:T(8,128)(2,1)S(1)}, u32[]{:S(2)}, u32[]{:S(2)}) collective-permute-start(bf16[8,272,128]{2,1,0:T(8,128)(2,1)S(1)} %maximum_dynamic-update-slice_fusion.refs_2_), channel_id=1, source_target_pairs={{0,32},{32,64},{64,96},{96,0},{1,33},{33,65},{65,97},{97,1},{2,34}... | collective-permute-start | bytes 1671176 | tf_op jit(solution)/shard_map/ppermute | solution.py:373
  23.6 11.5 %collective-permute-start = (bf16[8,272,128]{2,1,0:T(8,128)(2,1)S(1)}, bf16[8,272,128]{2,1,0:T(8,128)(2,1)S(1)}, u32[]{:S(2)}, u32[]{:S(2)}) collective-permute-start(bf16[8,272,128]{2,1,0:T(8,128)(2,1)S(1)} %maximum_dynamic-update-slice_fusion.refs_2_), channel_id=1, source_target_pairs={{0,96},{32,0},{64,32},{96,64},{1,97},{33,1},{65,33},{97,65},{2,98}... | collective-permute-start | bytes 1671176 | tf_op jit(solution)/shard_map/ppermute | solution.py:372
  31.9 6.6 %collective-permute-start.5 = (bf16[2304,128]{1,0:T(8,128)(2,1)S(1)}, bf16[2304,128]{1,0:T(8,128)(2,1)S(1)}, u32[]{:S(2)}, u32[]{:S(2)}) collective-permute-start(bf16[2304,128]{1,0:T(8,128)(2,1)S(1)} %collective-permute-done.2.refs_3_.refs_4_), channel_id=1, source_target_pairs={{0,8},{8,0},{1,9},{9,1},{2,10},{10,2},{3,11},{11,3},{4,12},{12,4},... | collective-permute-start | bytes 1769480 | tf_op jit(solution)/shard_map/ppermute | solution.py:383
  35.1 17.6 %collective-permute-start.4 = (bf16[8,272,128]{2,1,0:T(8,128)(2,1)S(1)}, bf16[8,272,128]{2,1,0:T(8,128)(2,1)S(1)}, u32[]{:S(2)}, u32[]{:S(2)}) collective-permute-start(bf16[8,272,128]{2,1,0:T(8,128)(2,1)S(1)} %maximum_dynamic-update-slice_fusion.refs_2_), channel_id=1, source_target_pairs={{0,64},{32,96},{64,0},{96,32},{1,65},{33,97},{65,1},{97,33},{2,66}... | collective-permute-start | bytes 1671176 | tf_op jit(solution)/shard_map/ppermute | solution.py:386
  55.8 3.4 %collective-permute-start.6 = (f32[256,1152]{1,0:T(8,128)S(1)}, f32[256,1152]{1,0:T(8,128)S(1)}, u32[]{:S(2)}, u32[]{:S(2)}) collective-permute-start(f32[256,1152]{1,0:T(8,128)S(1)} %get-tuple-element.78), channel_id=1, source_target_pairs={{0,8},{8,0},{1,9},{9,1},{2,10},{10,2},{3,11},{11,3},{4,12},{12,4},... | collective-permute-start | bytes 3538952 | tf_op jit(solution)/shard_map/ppermute | solution.py:391
  59.3 21.8 %collective-permute-start.7 = (bf16[256,1152]{1,0:T(8,128)(2,1)S(1)}, bf16[256,1152]{1,0:T(8,128)(2,1)S(1)}, u32[]{:S(2)}, u32[]{:S(2)}) collective-permute-start(bf16[256,1152]{1,0:T(8,128)(2,1)S(1)} %add_convert_fusion), channel_id=1, source_target_pairs={{0,16},{16,0},{1,17},{17,1},{2,18},{18,2},{3,19},{19,3},{4,20},{20... | collective-permute-start | bytes 1769480 | tf_op jit(solution)/shard_map/ppermute | solution.py:394
  80.9 6.1 %collective-permute-start.8 = (f32[256,1152]{1,0:T(8,128)}, f32[256,1152]{1,0:T(8,128)}, u32[]{:S(2)}, u32[]{:S(2)}) collective-permute-start(f32[256,1152]{1,0:T(8,128)} %get-tuple-element.88), channel_id=1, source_target_pairs={{0,8},{8,0},{1,9},{9,1},{2,10},{10,2},{3,11},{11,3},{4,12},{12,4},... | collective-permute-start | bytes 3538952 | tf_op jit(solution)/shard_map/ppermute | solution.py:402
  81.2 5.8 %copy-start.1 = (bf16[256,1152]{1,0:T(8,128)(2,1)}, bf16[256,1152]{1,0:T(8,128)(2,1)S(1)}, u32[]{:S(2)}) copy-start(bf16[256,1152]{1,0:T(8,128)(2,1)S(1)} %collective-permute-done.7.chip_in) | copy-start | bytes 1769476
  81.2 24.1 %all-to-all-start.1 = ((bf16[32,128,128]{2,1,0:T(8,128)(2,1)}), bf16[32,128,128]{2,1,0:T(8,128)(2,1)S(1)}, u32[]{:S(2)}, u32[]{:S(2)}) async-start(bf16[32,128,128]{2,1,0:T(8,128)(2,1)} %bitcast.9), calls=%async_computation.1 | async-start | bytes 2097152 | tf_op jit(solution)/shard_map/all_to_all | solution.py:405

commit v2 on v1

--- a/solution.py
+++ b/solution.py
@@ -64,10 +64,10 @@
         copy.wait()
     ones = jnp.ones((16, HD), BF16)
     row = lax.broadcasted_iota(jnp.int32, (16, BLOCK), 0)
-    for b in range(SRC):
+    def destination(b, carry):
         prods = []
         for h in range(GROUP):
-            cols = slice((b * GROUP + h) * HD, (b * GROUP + h + 1) * HD)
+            cols = pl.ds(pl.multiple_of(b * GROUP * HD, GROUP * HD) + h * HD, HD)
             qh, gh = q[:, cols], g[:, cols]
             pay[b, h * SUB : (h + 1) * SUB, :] = qh
             pay[b, BLOCK + h * SUB : BLOCK + (h + 1) * SUB, :] = gh
@@ -78,6 +78,9 @@
         d1, d2, d3 = pieces_of(dot(ones, high, NT) + dot(ones, low, NT))
         rows = jnp.where(row == 0, d1, jnp.where(row == 1, d2, jnp.where(row == 2, d3, 0.0)))
         pay[b, DROW:PAY, :] = rows.astype(BF16)
+        return carry
+
+    lax.fori_loop(0, SRC, destination, 0)
 
 
 def in_hbm(arrays):
@@ -188,7 +191,7 @@
 
     dq[...] = jnp.zeros((rows_all, HD), F32) if dq_in is None else dq_in[...]
     part = 256
-    steps = 2 if unit == "near" else 2 if nk == 2 else 1
+    steps = 1 if nk == 1 or blocks else 2 if have_sums[0] or unit != "own" else 4
 
     def step(n, carry):
         total = None
@@ -225,11 +228,11 @@
             @pl.when(seen)
             def _():
                 allowed = None
-                if unit == "own":
+                if unit == "own" and not other_chip and not other_core:
                     row = lax.broadcasted_iota(jnp.int32, (QR, RK), 0)
                     key_at = lax.broadcasted_iota(jnp.int32, (QR, RK), 1)
                     token = (row // BLOCK) * SUB + row % SUB
-                    allowed = (kj < qi) | (key_at <= token)
+                    allowed = key_at <= token
                 s, dp = products(j, PK, RK, QR)
                 dq[:QR, :] += grads(j, PK, RK, QR, s, dp, allowed, sums[j])
 
@@ -287,12 +290,16 @@
 
 
 def finish_kernel(parts, out):
-    for b in range(SRC):
+    def group(b, carry):
+        at = pl.multiple_of(b * GROUP * HD, GROUP * HD)
         for h in range(GROUP):
             rows = slice(h * SUB, (h + 1) * SUB)
             terms = [parts[n * SRC + b, rows, :].astype(F32) for n in range(4)]
-            col = (b * GROUP + h) * HD
-            out[:, col : col + HD] = (terms[0] + terms[1] + terms[2] + terms[3]).astype(BF16)
+            total = terms[0] + terms[1] + terms[2] + terms[3]
+            out[:, pl.ds(at + h * HD, HD)] = total.astype(BF16)
+        return carry
+
+    lax.fori_loop(0, SRC, group, 0)
 
 
 def finish(parts):

time: 106 us -> 107 us (level)
  starting transfers between devices: 25 us -> 22.5 us
  Pallas kernels: 57.4 us -> 59.8 us
    pallas_call x8, Pallas kernels: 48.9 us -> 50.4 us  [tiles(): pl.pallas_call(functools.partial(tiles_kernel, (unit, tuple(keys_of), hav...]
    all_to_all x1, starting transfers between devices: 5.76 us -> 4.66 us  [shards(): lax.all_to_all(dq, (Y,) + BULK, split_axis=0, concat_axis=0, tiled=True)]
  transfers between devices with their start and end apart: 11 -> 11, of which waited for: 2 -> 2; matrix products, arithmetic and copies ran while one was open for 0% -> 0% of each run, Pallas kernels for 48% -> 49%
where the time goes in v2:
time: 107 us
  Pallas kernels  59.8 us (56%)
  waiting for transfers between devices  22.7 us (21%)
  starting transfers between devices  22.5 us (21%)
    pallas_call x8, Pallas kernels, tiles(): pl.pallas_call(functools.partial(tiles_kernel, (unit, tuple(keys_of), hav...  50.4 us
    all_to_all x1, waiting for transfers between devices, shards(): lax.all_to_all(dq, (Y,) + BULK, split_axis=0, concat_axis=0, tiled=True)  15.1 us
    all_to_all x1, waiting for transfers between devices, shards(): own = lax.all_to_all(payload, BULK, split_axis=0, concat_axis=0, tiled=True)  7.62 us
    all_to_all x1, starting transfers between devices, shards(): own = lax.all_to_all(payload, BULK, split_axis=0, concat_axis=0, tiled=True)  6.34 us
    all_to_all x1, starting transfers between devices, shards(): lax.all_to_all(dq, (Y,) + BULK, split_axis=0, concat_axis=0, tiled=True)  4.66 us
    pallas_call x1, Pallas kernels, pack(): pl.pallas_call(pack_kernel, in_specs=[SSPEC] + [ANYSPEC] * 3, out_specs=V...  3.85 us
    pallas_call x1, Pallas kernels, close(): pl.pallas_call(close_kernel, in_specs=[VSPEC, VSPEC, ANYSPEC], out_specs=...  3.68 us
    ppermute x1, starting transfers between devices, shards(): opp = lax.ppermute(after(own, up, down), Y, shift(4, 2))  2.84 us
  transfers between devices with their start and end apart: 11, of which 2 were waited for; matrix products, arithmetic and copies ran while one was open for 0% of the time, Pallas kernels for 49%

profile of v2, /device:TPU:0, one launch (start us, length us, event | category | flops | bytes accessed | tf_op | source)
XLA Modules:
  0.0 106.5 jit_solution(8103306094637368216)
XLA Ops:
  0.7 3.8 %pack.1 = bf16[8,272,128]{2,1,0:T(8,128)(2,1)} custom-call(s32[3]{0:T(128)S(1)} %pad_add_fusion.place.refs_0_, bf16[16,8192]{1,0:T(8,128)(2,1)} %q_in.1, bf16[16,8192]{1,0:T(8,128)(2,1)} %g_in.1, bf16[16,8192]{1,0:T(8,128)(2,1)} %o_in.1), custom_call_target="tpu_custom_call" | custom-call | tf_op jit(solution)/shard_map/pack/pallas_call | solution.py:91
  4.6 6.3 %all-to-all-start = ((bf16[8,272,128]{2,1,0:T(8,128)(2,1)}), bf16[8,272,128]{2,1,0:T(8,128)(2,1)S(1)}, u32[]{:S(2)}, u32[]{:S(2)}) async-start(bf16[8,272,128]{2,1,0:T(8,128)(2,1)} %pack.1), calls=%async_computation | async-start | bytes 1114112 | tf_op jit(solution)/shard_map/all_to_all | solution.py:374
  10.9 1.1 %join.1.refs_3_.refs_4_ = bf16[2304,128]{1,0:T(8,128)(2,1)S(1)} custom-call(bf16[1024,128]{1,0:T(8,128)(2,1)} %pk, bf16[128,128]{1,0:T(8,128)(2,1)} %rk, bf16[1024,128]{1,0:T(8,128)(2,1)} %pv, bf16[128,128]{1,0:T(8,128)(2,1)} %rv), custom_call_target="tpu_custom_call" | custom-call | tf_op jit(solution)/shard_map/join/pallas_call | solution.py:115
  12.0 0.1 collective-permute-start.3
  12.1 2.8 %collective-permute-start.2 = (bf16[2304,128]{1,0:T(8,128)(2,1)S(1)}, bf16[2304,128]{1,0:T(8,128)(2,1)S(1)}, u32[]{:S(2)}, u32[]{:S(2)}) collective-permute-start(bf16[2304,128]{1,0:T(8,128)(2,1)S(1)} %join.1.refs_3_.refs_4_), channel_id=1, source_target_pairs={{0,16},{16,0},{1,17},{17,1},{2,18},{18,2},{3,19},{19,3},{4,20},{20... | collective-permute-start | bytes 1769480 | tf_op jit(solution)/shard_map/ppermute | solution.py:377
  15.2 7.6 %all-to-all-done = bf16[8,272,128]{2,1,0:T(8,128)(2,1)S(1)} async-done(((bf16[8,272,128]{2,1,0:T(8,128)(2,1)}), bf16[8,272,128]{2,1,0:T(8,128)(2,1)S(1)}, u32[]{:S(2)}, u32[]{:S(2)}) %all-to-all-start) | async-done | bytes 557088 | tf_op jit(solution)/shard_map/all_to_all | solution.py:374
  22.9 1.6 %collective-permute-start.1 = (bf16[8,272,128]{2,1,0:T(8,128)(2,1)S(1)}, bf16[8,272,128]{2,1,0:T(8,128)(2,1)S(1)}, u32[]{:S(2)}, u32[]{:S(2)}) collective-permute-start(bf16[8,272,128]{2,1,0:T(8,128)(2,1)S(1)} %maximum_dynamic-update-slice_fusion.refs_2_), channel_id=1, source_target_pairs={{0,32},{32,64},{64,96},{96,0},{1,33},{33,65},{65,97},{97,1},{2,34}... | collective-permute-start | bytes 1671176 | tf_op jit(solution)/shard_map/ppermute | solution.py:380
  24.5 1.7 %collective-permute-start = (bf16[8,272,128]{2,1,0:T(8,128)(2,1)S(1)}, bf16[8,272,128]{2,1,0:T(8,128)(2,1)S(1)}, u32[]{:S(2)}, u32[]{:S(2)}) collective-permute-start(bf16[8,272,128]{2,1,0:T(8,128)(2,1)S(1)} %maximum_dynamic-update-slice_fusion.refs_2_), channel_id=1, source_target_pairs={{0,96},{32,0},{64,32},{96,64},{1,97},{33,1},{65,33},{97,65},{2,98}... | collective-permute-start | bytes 1671176 | tf_op jit(solution)/shard_map/ppermute | solution.py:379
  26.2 7.0 %own_here.1 = (f32[256,1152]{1,0:T(8,128)S(1)}, f32[256,1152]{1,0:T(8,128)S(1)}, f32[1024,128]{1,0:T(8,128)S(1)}) custom-call(s32[3]{0:T(128)S(1)} %pad_add_fusion.place.refs_0_, s32[8]{0:T(128)S(1)} %copy-done, bf16[8,272,128]{2,1,0:T(8,128)(2,1)S(1)} %maximum_dynamic-update-slice_fusion.refs_2_, bf16[2304,128]{1,0:T(8,128)(2,1)S(1)} %join.1.refs_3_.refs_4_, ...), custom_call_target="tpu_custom_call" | custom-call | flops 1 | bytes 1 | tf_op jit(solution)/shard_map/own_here/pallas_call | solution.py:268
  33.3 3.1 %own_chip.1 = (f32[256,1152]{1,0:T(8,128)S(1)}, f32[1024,128]{1,0:T(8,128)S(1)}) custom-call(s32[3]{0:T(128)S(1)} %pad_add_fusion.place.refs_0_, s32[8]{0:T(128)S(1)} %copy-done, bf16[8,272,128]{2,1,0:T(8,128)(2,1)S(1)} %maximum_dynamic-update-slice_fusion.refs_2_, ...), custom_call_target="tpu_custom_call", output_to_operand_aliasing={{1}: (4, {})} | custom-call | flops 1 | bytes 1 | tf_op jit(solution)/shard_map/own_chip/pallas_call | solution.py:268
  36.4 2.8 %collective-permute-start.4 = (bf16[8,272,128]{2,1,0:T(8,128)(2,1)S(1)}, bf16[8,272,128]{2,1,0:T(8,128)(2,1)S(1)}, u32[]{:S(2)}, u32[]{:S(2)}) collective-permute-start(bf16[8,272,128]{2,1,0:T(8,128)(2,1)S(1)} %maximum_dynamic-update-slice_fusion.refs_2_), channel_id=1, source_target_pairs={{0,64},{32,96},{64,0},{96,32},{1,65},{33,97},{65,1},{97,33},{2,66}... | collective-permute-start | bytes 1671176 | tf_op jit(solution)/shard_map/ppermute | solution.py:393
  39.3 3.3 %own_both.1 = (f32[256,1152]{1,0:T(8,128)S(1)}, bf16[8,128,128]{2,1,0:T(8,128)(2,1)S(1)}) custom-call(s32[3]{0:T(128)S(1)} %pad_add_fusion.place.refs_0_, s32[8]{0:T(128)S(1)} %copy-done, bf16[8,272,128]{2,1,0:T(8,128)(2,1)S(1)} %maximum_dynamic-update-slice_fusion.refs_2_, bf16[2304,128]{1,0:T(8,128)(2,1)S(1)} %collective-permute-done.5.refs_3_.refs_5_, ...), custom_call_target="tpu_custom_call" | custom-call | flops 1 | bytes 1 | tf_op jit(solution)/shard_map/own_both/pallas_call | solution.py:268
  42.6 12.3 %near_far.1 = (f32[256,1152]{1,0:T(8,128)S(1)}, f32[256,1152]{1,0:T(8,128)S(1)}, f32[2048,128]{1,0:T(8,128)S(1)}) custom-call(s32[3]{0:T(128)S(1)} %pad_add_fusion.place.refs_0_, s32[8]{0:T(128)S(1)} %copy-done, bf16[8,272,128]{2,1,0:T(8,128)(2,1)S(1)} %collective-permute-done.refs_2_, ...), custom_call_target="tpu_custom_call", output_to_operand_aliasing={{0}: (6, {}), {1}: (7, {})} | custom-call | flops 1 | bytes 1 | tf_op jit(solution)/shard_map/near_far/pallas_call | solution.py:268
  54.9 3.1 %opp_both.1 = (f32[256,1152]{1,0:T(8,128)S(1)}, f32[1024,128]{1,0:T(8,128)S(1)}) custom-call(s32[3]{0:T(128)S(1)} %pad_add_fusion.place.refs_0_, s32[8]{0:T(128)S(1)} %copy-done, bf16[8,272,128]{2,1,0:T(8,128)(2,1)S(1)} %collective-permute-done.4.refs_2_, ...), custom_call_target="tpu_custom_call", output_to_operand_aliasing={{0}: (4, {})} | custom-call | flops 1 | bytes 1 | tf_op jit(solution)/shard_map/opp_both/pallas_call | solution.py:268
  58.0 3.1 %opp_chip.1 = (f32[256,1152]{1,0:T(8,128)S(1)}, f32[1024,128]{1,0:T(8,128)S(1)}) custom-call(s32[3]{0:T(128)S(1)} %pad_add_fusion.place.refs_0_, s32[8]{0:T(128)S(1)} %copy-done, bf16[8,272,128]{2,1,0:T(8,128)(2,1)S(1)} %collective-permute-done.4.refs_2_, ...), custom_call_target="tpu_custom_call", output_to_operand_aliasing={{0}: (4, {}), {1}: (5, {})} | custom-call | flops 1 | bytes 1 | tf_op jit(solution)/shard_map/opp_chip/pallas_call | solution.py:268
  61.1 0.1 add_convert_fusion
  61.3 2.3 %collective-permute-start.7 = (bf16[256,1152]{1,0:T(8,128)(2,1)S(1)}, bf16[256,1152]{1,0:T(8,128)(2,1)S(1)}, u32[]{:S(2)}, u32[]{:S(2)}) collective-permute-start(bf16[256,1152]{1,0:T(8,128)(2,1)S(1)} %add_convert_fusion), channel_id=1, source_target_pairs={{0,16},{16,0},{1,17},{17,1},{2,18},{18,2},{3,19},{19,3},{4,20},{20... | collective-permute-start | bytes 1769480 | tf_op jit(solution)/shard_map/ppermute | solution.py:401
  63.5 11.5 %near_here.1 = (f32[256,1152]{1,0:T(8,128)S(1)}, f32[256,1152]{1,0:T(8,128)S(1)}, bf16[2,8,128,128]{3,2,1,0:T(8,128)(2,1)S(1)}) custom-call(s32[3]{0:T(128)S(1)} %pad_add_fusion.place.refs_0_, s32[8]{0:T(128)S(1)} %copy-done, bf16[8,272,128]{2,1,0:T(8,128)(2,1)S(1)} %collective-permute-done.refs_2_, ...), custom_call_target="tpu_custom_call", output_to_operand_aliasing={{0}: (6, {}), {1}: (7, {})} | custom-call | flops 1 | bytes 1 | tf_op jit(solution)/shard_map/near_here/pallas_call | solution.py:268
  75.0 7.0 %opp_here.1 = (f32[256,1152]{1,0:T(8,128)S(1)}, f32[256,1152]{1,0:T(8,128)}, bf16[4,8,128,128]{3,2,1,0:T(8,128)(2,1)}) custom-call(s32[3]{0:T(128)S(1)} %pad_add_fusion.place.refs_0_, s32[8]{0:T(128)S(1)} %copy-done, bf16[8,272,128]{2,1,0:T(8,128)(2,1)S(1)} %collective-permute-done.4.refs_2_, bf16[2304,128]{1,0:T(8,128)(2,1)S(1)} %join.1.refs_3_.refs_4_, ...), custom_call_target="tpu_custom_call" | custom-call | flops 1 | bytes 1 | tf_op jit(solution)/shard_map/opp_here/pallas_call | solution.py:268
  82.1 0.1 collective-permute-start.8
  82.2 4.7 %all-to-all-start.1 = ((bf16[32,128,128]{2,1,0:T(8,128)(2,1)}), bf16[32,128,128]{2,1,0:T(8,128)(2,1)S(1)}, u32[]{:S(2)}, u32[]{:S(2)}) async-start(bf16[32,128,128]{2,1,0:T(8,128)(2,1)} %bitcast.9), calls=%async_computation.1 | async-start | bytes 2097152 | tf_op jit(solution)/shard_map/all_to_all | solution.py:412
  86.9 3.7 %close.1 = (f32[1024,128]{1,0:T(8,128)}, f32[1024,128]{1,0:T(8,128)}, f32[128,128]{1,0:T(8,128)}, f32[128,128]{1,0:T(8,128)}) custom-call(f32[256,1152]{1,0:T(8,128)S(1)} %get-tuple-element.87.own, f32[256,1152]{1,0:T(8,128)} %collective-permute-done.8.core, bf16[256,1152]{1,0:T(8,128)(2,1)} %copy-done.1), custom_call_target="tpu_custom_call" | custom-call | tf_op jit(solution)/shard_map/close/pallas_call | solution.py:333
  90.6 15.1 %all-to-all-done.1.parts = bf16[32,128,128]{2,1,0:T(8,128)(2,1)S(1)} async-done(((bf16[32,128,128]{2,1,0:T(8,128)(2,1)}), bf16[32,128,128]{2,1,0:T(8,128)(2,1)S(1)}, u32[]{:S(2)}, u32[]{:S(2)}) %all-to-all-start.1) | async-done | bytes 1048608 | tf_op jit(solution)/shard_map/all_to_all | solution.py:412
  105.6 0.9 finish.1
  (26 shorter events, 0.6 us)
Async XLA Ops:
  4.6 10.4 %copy-start.2 = (f32[128,8]{0,1:T(8,128)S(1)}, f32[128,8]{0,1:T(8,128)}, u32[]{:S(2)}) copy-start(f32[128,8]{0,1:T(8,128)} %param.14) | copy-start | bytes 12292
  4.6 21.6 %copy-start = (s32[8]{0:T(128)S(1)}, s32[8]{0:T(128)}, u32[]{:S(2)}) copy-start(s32[8]{0:T(128)} %refs_1_.15) | copy-start | bytes 100
  4.6 18.2 %all-to-all-start = ((bf16[8,272,128]{2,1,0:T(8,128)(2,1)}), bf16[8,272,128]{2,1,0:T(8,128)(2,1)S(1)}, u32[]{:S(2)}, u32[]{:S(2)}) async-start(bf16[8,272,128]{2,1,0:T(8,128)(2,1)} %pack.1), calls=%async_computation | async-start | bytes 1114112 | tf_op jit(solution)/shard_map/all_to_all | solution.py:374
  12.0 14.2 %collective-permute-start.3 = (bf16[2304,128]{1,0:T(8,128)(2,1)S(1)}, bf16[2304,128]{1,0:T(8,128)(2,1)S(1)}, u32[]{:S(2)}, u32[]{:S(2)}) collective-permute-start(bf16[2304,128]{1,0:T(8,128)(2,1)S(1)} %join.1.refs_3_.refs_4_), channel_id=1, source_target_pairs={{0,8},{8,0},{1,9},{9,1},{2,10},{10,2},{3,11},{11,3},{4,12},{12,4},... | collective-permute-start | bytes 1769480 | tf_op jit(solution)/shard_map/ppermute | solution.py:376
  12.1 21.1 %collective-permute-start.2 = (bf16[2304,128]{1,0:T(8,128)(2,1)S(1)}, bf16[2304,128]{1,0:T(8,128)(2,1)S(1)}, u32[]{:S(2)}, u32[]{:S(2)}) collective-permute-start(bf16[2304,128]{1,0:T(8,128)(2,1)S(1)} %join.1.refs_3_.refs_4_), channel_id=1, source_target_pairs={{0,16},{16,0},{1,17},{17,1},{2,18},{18,2},{3,19},{19,3},{4,20},{20... | collective-permute-start | bytes 1769480 | tf_op jit(solution)/shard_map/ppermute | solution.py:377
  22.9 13.5 %collective-permute-start.1 = (bf16[8,272,128]{2,1,0:T(8,128)(2,1)S(1)}, bf16[8,272,128]{2,1,0:T(8,128)(2,1)S(1)}, u32[]{:S(2)}, u32[]{:S(2)}) collective-permute-start(bf16[8,272,128]{2,1,0:T(8,128)(2,1)S(1)} %maximum_dynamic-update-slice_fusion.refs_2_), channel_id=1, source_target_pairs={{0,32},{32,64},{64,96},{96,0},{1,33},{33,65},{65,97},{97,1},{2,34}... | collective-permute-start | bytes 1671176 | tf_op jit(solution)/shard_map/ppermute | solution.py:380
  24.5 11.9 %collective-permute-start = (bf16[8,272,128]{2,1,0:T(8,128)(2,1)S(1)}, bf16[8,272,128]{2,1,0:T(8,128)(2,1)S(1)}, u32[]{:S(2)}, u32[]{:S(2)}) collective-permute-start(bf16[8,272,128]{2,1,0:T(8,128)(2,1)S(1)} %maximum_dynamic-update-slice_fusion.refs_2_), channel_id=1, source_target_pairs={{0,96},{32,0},{64,32},{96,64},{1,97},{33,1},{65,33},{97,65},{2,98}... | collective-permute-start | bytes 1671176 | tf_op jit(solution)/shard_map/ppermute | solution.py:379
  33.2 6.1 %collective-permute-start.5 = (bf16[2304,128]{1,0:T(8,128)(2,1)S(1)}, bf16[2304,128]{1,0:T(8,128)(2,1)S(1)}, u32[]{:S(2)}, u32[]{:S(2)}) collective-permute-start(bf16[2304,128]{1,0:T(8,128)(2,1)S(1)} %collective-permute-done.2.refs_3_.refs_4_), channel_id=1, source_target_pairs={{0,8},{8,0},{1,9},{9,1},{2,10},{10,2},{3,11},{11,3},{4,12},{12,4},... | collective-permute-start | bytes 1769480 | tf_op jit(solution)/shard_map/ppermute | solution.py:390
  36.4 18.4 %collective-permute-start.4 = (bf16[8,272,128]{2,1,0:T(8,128)(2,1)S(1)}, bf16[8,272,128]{2,1,0:T(8,128)(2,1)S(1)}, u32[]{:S(2)}, u32[]{:S(2)}) collective-permute-start(bf16[8,272,128]{2,1,0:T(8,128)(2,1)S(1)} %maximum_dynamic-update-slice_fusion.refs_2_), channel_id=1, source_target_pairs={{0,64},{32,96},{64,0},{96,32},{1,65},{33,97},{65,1},{97,33},{2,66}... | collective-permute-start | bytes 1671176 | tf_op jit(solution)/shard_map/ppermute | solution.py:393
  57.9 3.2 %collective-permute-start.6 = (f32[256,1152]{1,0:T(8,128)S(1)}, f32[256,1152]{1,0:T(8,128)S(1)}, u32[]{:S(2)}, u32[]{:S(2)}) collective-permute-start(f32[256,1152]{1,0:T(8,128)S(1)} %get-tuple-element.78), channel_id=1, source_target_pairs={{0,8},{8,0},{1,9},{9,1},{2,10},{10,2},{3,11},{11,3},{4,12},{12,4},... | collective-permute-start | bytes 3538952 | tf_op jit(solution)/shard_map/ppermute | solution.py:398
  61.3 20.9 %collective-permute-start.7 = (bf16[256,1152]{1,0:T(8,128)(2,1)S(1)}, bf16[256,1152]{1,0:T(8,128)(2,1)S(1)}, u32[]{:S(2)}, u32[]{:S(2)}) collective-permute-start(bf16[256,1152]{1,0:T(8,128)(2,1)S(1)} %add_convert_fusion), channel_id=1, source_target_pairs={{0,16},{16,0},{1,17},{17,1},{2,18},{18,2},{3,19},{19,3},{4,20},{20... | collective-permute-start | bytes 1769480 | tf_op jit(solution)/shard_map/ppermute | solution.py:401
  82.1 4.8 %collective-permute-start.8 = (f32[256,1152]{1,0:T(8,128)}, f32[256,1152]{1,0:T(8,128)}, u32[]{:S(2)}, u32[]{:S(2)}) collective-permute-start(f32[256,1152]{1,0:T(8,128)} %get-tuple-element.88), channel_id=1, source_target_pairs={{0,8},{8,0},{1,9},{9,1},{2,10},{10,2},{3,11},{11,3},{4,12},{12,4},... | collective-permute-start | bytes 3538952 | tf_op jit(solution)/shard_map/ppermute | solution.py:409
  82.2 4.7 %copy-start.1 = (bf16[256,1152]{1,0:T(8,128)(2,1)}, bf16[256,1152]{1,0:T(8,128)(2,1)S(1)}, u32[]{:S(2)}) copy-start(bf16[256,1152]{1,0:T(8,128)(2,1)S(1)} %collective-permute-done.7.chip_in) | copy-start | bytes 1769476
  82.2 23.4 %all-to-all-start.1 = ((bf16[32,128,128]{2,1,0:T(8,128)(2,1)}), bf16[32,128,128]{2,1,0:T(8,128)(2,1)S(1)}, u32[]{:S(2)}, u32[]{:S(2)}) async-start(bf16[32,128,128]{2,1,0:T(8,128)(2,1)} %bitcast.9), calls=%async_computation.1 | async-start | bytes 2097152 | tf_op jit(solution)/shard_map/all_to_all | solution.py:412
